TPU v7x, 32 devices: a whole 2x2x4 slice. The times are simulated.
32 devices in a mesh: test: 4 (over y, core), src: 8 (over z, x).
Axes of the slice: x: 2, y: 2, z: 4, core: 2. Of those that a mesh axis runs over, the one named last changes fastest.
Arguments:
- test_points: float32 [8, 3, 1024], P('test'), may hold values from 0 to 1
- test_basis: bfloat16 [8, 1024, 384], P('test'), may hold values from -0.1875 to 0.1875
- test_counts: int32 [8], P('test'), may hold values from 128 to 384, as said below
- source_points: float32 [64, 3, 1024], P('src'), may hold values from 0 to 1
- source_basis: bfloat16 [64, 1024, 384], P('src', 'test'), may hold values from -0.1875 to 0.1875
- source_counts: int32 [64], P('src'), may hold values from 128 to 384, as said below
- coefficients: bfloat16 [64, 384, 512], P('src'), may hold values from -0.0546875 to 0.0546875
Outputs:
- reduced: bfloat16 [8, 384, 64, 384], P('test', 'src')
- projected: bfloat16 [8, 384, 512], P('test', 'src')
Inputs may be any that keep to these rules, and one draw needn't show every extreme that they name: `test_counts`: number of leading basis columns of a test block that are used; the rest are ignored. Some test block uses all 384 in every draw. `source_counts`: number of leading basis columns of a source block that are used; the rest are ignored. Some source block uses all 384 in every draw.
All inputs are finite; a program needn't handle non-finite values.
Results may differ from a plain program's by a relative error of at most 0.015.
Values may be sent and summed in bfloat16 or wider, within the bound.
No kernel may reach another device: no remote copies, remote signals or barrier semaphores. Data moves between devices by JAX's collectives and lax.ppermute only.
A program may use at most 128 MiB of HBM per device.

v0:
```python
import functools

import jax
import jax.numpy as jnp
from jax import lax
from jax.experimental import pallas as pl
from jax.experimental.pallas import tpu as pltpu
from jax.sharding import PartitionSpec as P

softening = 0.0025
QBLOCK = 256
VMEM_LIMIT = 40 * 1024 * 1024


def exchange(x, axis, flip):
    size = lax.axis_size(axis)
    return lax.ppermute(x, axis, [(a, a ^ flip) for a in range(size)])


def bits_down(size):
    bit = size // 2
    while bit >= 1:
        yield bit
        bit //= 2


def gather_shards(shard, axis):
    held = {0: shard}
    for bit in bits_down(lax.axis_size(axis)):
        for offset in list(held):
            held[offset ^ bit] = exchange(held[offset], axis, bit)
    return [held[offset] for offset in sorted(held)]


def sum_rows(total, axis):
    me = lax.axis_index(axis)
    bits = list(bits_down(lax.axis_size(axis)))
    held = total.reshape((2,) * len(bits) + total.shape[1:])
    for bit in [bits[-1]] + bits[:-1]:
        place = len(bits) - 1 if bit == 1 else 0
        mine = (me // bit) % 2
        keep = lax.dynamic_index_in_dim(held, mine, place, keepdims=False)
        give = lax.dynamic_index_in_dim(held, 1 - mine, place, keepdims=False)
        got = exchange(give.astype(jnp.bfloat16), axis, bit)
        held = keep + got.astype(jnp.float32)
        bits = [b for b in bits if b != bit]
    return held


def left_kernel(test_ref, source_ref, basis_ref, out_ref):
    nq = source_ref.shape[2]
    block = min(QBLOCK, nq)
    for start in range(0, nq, block):
        total = None
        for comp in range(3):
            delta = test_ref[0, :, comp : comp + 1] - source_ref[0, comp : comp + 1, start : start + block]
            total = delta * delta if total is None else total + delta * delta
        kernel = lax.rsqrt(total + softening).astype(jnp.bfloat16)
        out_ref[0, 0, :, start : start + block] = jnp.dot(
            basis_ref[0], kernel, preferred_element_type=jnp.float32
        ).astype(jnp.bfloat16)


def left_products(test_columns, source_points, basis_rows):
    ntest, npoint, _ = test_columns.shape
    nsource, _, nq = source_points.shape
    kmax = basis_rows.shape[1]
    return pl.pallas_call(
        left_kernel,
        grid=(ntest, nsource),
        out_shape=jax.ShapeDtypeStruct((ntest, nsource, kmax, nq), jnp.bfloat16),
        in_specs=[
            pl.BlockSpec((1, npoint, 3), lambda i, j: (i, 0, 0)),
            pl.BlockSpec((1, 3, nq), lambda i, j: (j, 0, 0)),
            pl.BlockSpec((1, kmax, npoint), lambda i, j: (i, 0, 0)),
        ],
        out_specs=pl.BlockSpec((1, 1, kmax, nq), lambda i, j: (i, j, 0, 0)),
        compiler_params=pltpu.CompilerParams(vmem_limit_bytes=VMEM_LIMIT),
        cost_estimate=pl.CostEstimate(
            flops=2 * ntest * nsource * npoint * nq * kmax,
            bytes_accessed=2 * ntest * nsource * kmax * nq,
            transcendentals=ntest * nsource * npoint * nq,
        ),
    )(test_columns, source_points, basis_rows)


def tile_kernel(nshard, ndest, test_counts_ref, source_counts_ref, left_ref, *refs):
    shard_refs, coeff_ref, tile_ref, sum_ref = refs[:nshard], refs[nshard], refs[-2], refs[-1]
    i, j = pl.program_id(0), pl.program_id(1)
    kmax = left_ref.shape[2]
    part = left_ref.shape[3] // nshard
    tile = None
    for place, shard_ref in enumerate(shard_refs):
        term = jnp.dot(
            left_ref[0, 0, :, place * part : (place + 1) * part],
            shard_ref[0],
            preferred_element_type=jnp.float32,
        )
        tile = term if tile is None else tile + term
    row_ids = lax.broadcasted_iota(jnp.int32, tile.shape, 0)
    column_ids = lax.broadcasted_iota(jnp.int32, tile.shape, 1)
    used = (row_ids < test_counts_ref[i]) & (column_ids < source_counts_ref[j])
    tile = jnp.where(used, tile, 0.0)
    rows = kmax // ndest
    for dest in range(ndest):
        tile_ref[dest, 0, 0] = tile[dest * rows : (dest + 1) * rows].astype(jnp.bfloat16)
    term = jnp.dot(tile.astype(jnp.bfloat16), coeff_ref[0], preferred_element_type=jnp.float32)

    @pl.when(j == 0)
    def _():
        sum_ref[0] = term

    @pl.when(j > 0)
    def _():
        sum_ref[0] += term


def tiles_and_sums(ndest, test_counts, source_counts, left, shards, coefficients):
    ntest, nsource, kmax, nq = left.shape
    nshard = len(shards)
    part, width = shards[0].shape[1:]
    ncol = coefficients.shape[2]
    rows = kmax // ndest
    smem = pl.BlockSpec(memory_space=pltpu.SMEM)
    return pl.pallas_call(
        functools.partial(tile_kernel, nshard, ndest),
        grid=(ntest, nsource),
        out_shape=(
            jax.ShapeDtypeStruct((ndest, ntest, nsource, rows, width), jnp.bfloat16),
            jax.ShapeDtypeStruct((ntest, kmax, ncol), jnp.float32),
        ),
        in_specs=[smem, smem, pl.BlockSpec((1, 1, kmax, nq), lambda i, j: (i, j, 0, 0))]
        + [pl.BlockSpec((1, part, width), lambda i, j: (j, 0, 0))] * nshard
        + [pl.BlockSpec((1, kmax, ncol), lambda i, j: (j, 0, 0))],
        out_specs=(
            pl.BlockSpec((ndest, 1, 1, rows, width), lambda i, j: (0, i, j, 0, 0)),
            pl.BlockSpec((1, kmax, ncol), lambda i, j: (i, 0, 0)),
        ),
        compiler_params=pltpu.CompilerParams(vmem_limit_bytes=VMEM_LIMIT),
        cost_estimate=pl.CostEstimate(
            flops=2 * ntest * nsource * kmax * width * (nq + ncol),
            bytes_accessed=2 * ntest * nsource * kmax * (nq + width),
            transcendentals=0,
        ),
    )(test_counts, source_counts, left, *shards, coefficients)


def body(
    test_points, test_basis, test_counts, source_points, source_basis, source_counts, coefficients
):
    nsource, part, kmax = source_basis.shape
    ntest = test_points.shape[0]
    ncol = coefficients.shape[2]
    nsrc = lax.axis_size("src")
    ntest_axis = lax.axis_size("test")
    rows = kmax // nsrc
    me_test = lax.axis_index("test")
    points = jnp.concatenate(
        [
            lax.dynamic_slice_in_dim(source_points, (me_test ^ offset) * part, part, 2)
            for offset in range(ntest_axis)
        ],
        axis=2,
    )
    test_columns = test_points.transpose(0, 2, 1)
    basis_rows = test_basis.transpose(0, 2, 1)
    cut = max(1, nsource // 4)
    first_shards = gather_shards(source_basis[:cut], "test")
    rest, _ = lax.optimization_barrier((source_basis[cut:], first_shards[ntest_axis // 2]))
    rest_shards = gather_shards(rest, "test")
    groups = [(0, cut, first_shards), (cut, nsource, rest_shards)]
    moved = []
    total = 0.0
    for first, last, shards in groups:
        left = left_products(test_columns, points[first:last], basis_rows)
        tiles, sums = tiles_and_sums(
            nsrc, test_counts, source_counts[first:last], left, shards, coefficients[first:last]
        )
        total = total + sums
        moved.append(lax.all_to_all(tiles, "src", split_axis=0, concat_axis=0, tiled=True))
    reduced = jnp.concatenate(moved, axis=2).transpose(1, 3, 0, 2, 4)
    reduced = reduced.reshape(ntest, rows, nsrc * nsource, kmax)
    summed = total.reshape(ntest, nsrc, rows, ncol).transpose(1, 0, 2, 3)
    projected = sum_rows(summed, "src").astype(jnp.bfloat16)
    return (reduced, projected)


def solution(mesh):
    return jax.shard_map(
        body,
        mesh=mesh,
        in_specs=(
            P("test", None, None),
            P("test", None, None),
            P("test"),
            P("src", None, None),
            P("src", "test", None),
            P("src"),
            P("src", None, None),
        ),
        out_specs=(P("test", "src", None, None), P("test", "src", None)),
        check_vma=False,
    )
```

profile of v0, /device:TPU:0, one launch (start us, length us, event | category | flops | bytes accessed | tf_op | source)
XLA Modules:
  0.0 198.8 jit_solution(17701429294124019824)
XLA Ops:
  0.6 1.1 slice.26.refs_0_
  1.7 3.0 %collective-permute-start.1 = (bf16[2,256,384]{2,1,0:T(8,128)(2,1)S(1)}, bf16[2,256,384]{2,1,0:T(8,128)(2,1)S(1)}, u32[]{:S(2)}, u32[]{:S(2)}) collective-permute-start(bf16[2,256,384]{2,1,0:T(8,128)(2,1)S(1)} %slice.26.refs_0_), channel_id=1, source_target_pairs={{0,16},{8,24},{16,0},{24,8},{1,17},{9,25},{17,1},{25,9},{2,18},{10... | collective-permute-start | bytes 1179656 | tf_op jit(solution)/shard_map/ppermute | solution.py:17
  4.7 0.0 collective-permute-start
  4.7 2.4 %slice.30.refs_0_ = bf16[6,256,384]{2,1,0:T(8,128)(2,1)} slice(bf16[8,256,384]{2,1,0:T(8,128)(2,1)} %param.11), slice={[2:8], [0:256], [0:384]} | slice | bytes 2359296 | tf_op jit(solution)/shard_map/slice | solution.py:169
  7.2 6.6 %collective-permute-done.1.refs_2_ = bf16[2,256,384]{2,1,0:T(8,128)(2,1)S(1)} collective-permute-done((bf16[2,256,384]{2,1,0:T(8,128)(2,1)S(1)}, bf16[2,256,384]{2,1,0:T(8,128)(2,1)S(1)}, u32[]{:S(2)}, u32[]{:S(2)}) %collective-permute-start.1) | collective-permute-done | bytes 393248 | tf_op jit(solution)/shard_map/ppermute | solution.py:17
  13.9 1.7 collective-permute-start.4
  15.6 0.1 collective-permute-start.2
  15.7 0.6 copy-done.9
  16.4 2.1 %slice.27.refs_4_ = bf16[2,384,512]{2,1,0:T(8,128)(2,1)} slice(bf16[8,384,512]{2,1,0:T(8,128)(2,1)} %param.13), slice={[0:2], [0:384], [0:512]} | slice | bytes 1572864 | tf_op jit(solution)/shard_map/slice | solution.py:177
  18.5 0.4 copy.15
  18.8 0.0 copy-start.1
  18.8 2.1 %copy.20 = bf16[2,1024,384]{1,2,0:T(8,128)(2,1)S(1)} copy(bf16[2,1024,384]{2,1,0:T(8,128)(2,1)} %param.8) | data formatting | bytes 3145728 | tf_op args[1]
  21.0 0.0 copy-start.6
  21.0 0.0 copy-start.7
  21.0 9.2 %shard_map.86.left_ref = bf16[2,2,384,1024]{3,2,1,0:T(8,128)(2,1)S(1)} custom-call(f32[2,1024,3]{2,1,0:T(8,128)S(1)} %bitcast.28, f32[2,3,1024]{2,1,0:T(4,128)S(1)} %slice.32.source_ref, bf16[2,384,1024]{2,1,0:T(8,128)(2,1)S(1)} %bitcast.26), custom_call_target="tpu_custom_call" | custom-call | flops 3221225472 | bytes 3145728 | tf_op jit(solution)/shard_map/pallas_call | solution.py:68
  30.2 0.0 collective-permute-done.refs_1_
  30.2 0.0 collective-permute-done.2.refs_3_
  30.3 4.9 %shard_map.87 = (bf16[8,2,2,48,384]{4,3,2,1,0:T(8,128)(2,1)S(1)}, f32[2,384,512]{2,1,0:T(8,128)S(1)}) custom-call(s32[2]{0:T(128)S(1)} %copy-done.7, s32[2]{0:T(128)S(1)} %bitcast.30, bf16[2,2,384,1024]{3,2,1,0:T(8,128)(2,1)S(1)} %shard_map.86.left_ref, bf16[2,256,384]{2,1,0:T(8,128)(2,1)S(1)} %slice.26.refs_0_, ...), custom_call_target="tpu_custom_call" | custom-call | flops 1811939328 | bytes 4325376 | tf_op jit(solution)/shard_map/pallas_call | solution.py:125
  35.2 1.0 copy-done
  36.2 5.9 %all-to-all-start = ((bf16[8,2,2,48,384]{4,3,2,1,0:T(8,128)(2,1)}), bf16[8,2,2,48,384]{4,3,2,1,0:T(8,128)(2,1)}, u32[]{:S(2)}, u32[]{:S(2)}) async-start(bf16[8,2,2,48,384]{4,3,2,1,0:T(8,128)(2,1)} %copy-done), calls=%async_computation | async-start | bytes 2359296 | tf_op jit(solution)/shard_map/all_to_all | solution.py:180
  42.2 0.2 collective-permute-start.3
  42.4 0.0 collective-permute-done.4.refs_2_
  42.4 0.3 collective-permute-start.5
  42.7 0.1 slice.28.source_counts_ref
  42.8 0.0 copy-start.2
  42.8 1.9 slice.31.refs_4_
  44.7 0.0 copy-done.2
  44.7 29.3 %shard_map.88.left_ref = bf16[2,6,384,1024]{3,2,1,0:T(8,128)(2,1)S(1)} custom-call(f32[2,1024,3]{2,1,0:T(8,128)S(1)} %bitcast.29, f32[6,3,1024]{2,1,0:T(4,128)S(1)} %slice.33.source_ref, bf16[2,384,1024]{2,1,0:T(8,128)(2,1)S(1)} %bitcast.27), custom_call_target="tpu_custom_call" | custom-call | flops 9663676416 | bytes 9437184 | tf_op jit(solution)/shard_map/pallas_call | solution.py:68
  74.1 3.7 %copy-done.8 = bf16[2,6,384,1024]{3,2,1,0:T(8,128)(2,1)} copy-done((bf16[2,6,384,1024]{3,2,1,0:T(8,128)(2,1)}, bf16[2,6,384,1024]{3,2,1,0:T(8,128)(2,1)S(1)}, u32[]{:S(2)}) %copy-start.8) | copy-done | bytes 9437208
  77.7 0.0 collective-permute-done.3.refs_1_
  77.7 0.0 collective-permute-done.5.refs_3_
  77.7 15.5 %shard_map.89 = (bf16[8,2,6,48,384]{4,3,2,1,0:T(8,128)(2,1)}, f32[2,384,512]{2,1,0:T(8,128)S(1)}) custom-call(s32[2]{0:T(128)S(1)} %copy-done.7, s32[6]{0:T(128)S(1)} %slice.28.source_counts_ref, bf16[2,6,384,1024]{3,2,1,0:T(8,128)(2,1)} %copy-done.8, bf16[6,256,384]{2,1,0:T(8,128)(2,1)} %slice.30.refs_0_, ...), custom_call_target="tpu_custom_call" | custom-call | flops 5435817984 | bytes 12976128 | tf_op jit(solution)/shard_map/pallas_call | solution.py:125
  93.2 0.0 all-to-all-done
  93.3 6.0 %all-to-all-start.1 = ((bf16[8,2,6,48,384]{4,3,2,1,0:T(8,128)(2,1)}), bf16[8,2,6,48,384]{4,3,2,1,0:T(8,128)(2,1)}, u32[]{:S(2)}, u32[]{:S(2)}) async-start(bf16[8,2,6,48,384]{4,3,2,1,0:T(8,128)(2,1)} %get-tuple-element.9), calls=%async_computation.1 | async-start | bytes 7077888 | tf_op jit(solution)/shard_map/all_to_all | solution.py:180
  99.3 0.3 add.65
  99.6 0.1 copy.22
  99.8 0.1 fusion
  99.8 2.1 %collective-permute-start.6 = (bf16[2,2,2,48,512]{4,3,2,1,0:T(8,128)(2,1)S(1)}, bf16[2,2,2,48,512]{4,3,2,1,0:T(8,128)(2,1)S(1)}, u32[]{:S(2)}, u32[]{:S(2)}) collective-permute-start(bf16[2,2,2,48,512]{4,3,2,1,0:T(8,128)(2,1)S(1)} %fusion), channel_id=1, source_target_pairs={{0,1},{1,0},{2,3},{3,2},{4,5},{5,4},{6,7},{7,6},{8,9},{9,8},{10,11... | collective-permute-start | bytes 1179656 | tf_op jit(solution)/shard_map/ppermute | solution.py:17
  101.9 35.7 %collective-permute-done.6 = bf16[2,2,2,48,512]{4,3,2,1,0:T(8,128)(2,1)S(1)} collective-permute-done((bf16[2,2,2,48,512]{4,3,2,1,0:T(8,128)(2,1)S(1)}, bf16[2,2,2,48,512]{4,3,2,1,0:T(8,128)(2,1)S(1)}, u32[]{:S(2)}, u32[]{:S(2)}) %collective-permute-start.6) | collective-permute-done | bytes 393248 | tf_op jit(solution)/shard_map/ppermute | solution.py:17
  137.6 0.1 bitcast_add_fusion
  137.8 1.6 collective-permute-start.7
  139.4 47.7 %collective-permute-done.7 = bf16[2,2,48,512]{3,2,1,0:T(8,128)(2,1)S(1)} collective-permute-done((bf16[2,2,48,512]{3,2,1,0:T(8,128)(2,1)S(1)}, bf16[2,2,48,512]{3,2,1,0:T(8,128)(2,1)S(1)}, u32[]{:S(2)}, u32[]{:S(2)}) %collective-permute-start.7) | collective-permute-done | bytes 196640 | tf_op jit(solution)/shard_map/ppermute | solution.py:17
  187.1 0.1 collective-permute-start.8
  187.2 4.6 %collective-permute-done.8 = bf16[2,48,512]{2,1,0:T(8,128)(2,1)S(1)} collective-permute-done((bf16[2,48,512]{2,1,0:T(8,128)(2,1)S(1)}, bf16[2,48,512]{2,1,0:T(8,128)(2,1)S(1)}, u32[]{:S(2)}, u32[]{:S(2)}) %collective-permute-start.8) | collective-permute-done | bytes 98336 | tf_op jit(solution)/shard_map/ppermute | solution.py:17
  191.8 0.7 fusion.2
  192.5 0.0 all-to-all-done.1
  192.5 2.9 %maximum_bitcast_fusion = bf16[2,48,8,8,384]{4,1,3,0,2:T(8,128)(2,1)S(1)} fusion(bf16[8,2,6,48,384]{4,3,2,1,0:T(8,128)(2,1)} %all-to-all-done.1, bf16[8,2,2,48,384]{4,3,2,1,0:T(8,128)(2,1)} %all-to-all-done), kind=kLoop, calls=%fused_computation | loop fusion | flops 2359296 | bytes 9437184 | tf_op jit(solution)/shard_map/transpose | solution.py:181
  195.3 3.4 %copy.32 = bf16[2,48,8,8,384]{4,3,2,1,0:T(8,128)(2,1)} copy(bf16[2,48,8,8,384]{4,1,3,0,2:T(8,128)(2,1)S(1)} %maximum_bitcast_fusion) | data formatting | bytes 9437184 | tf_op jit(solution)/shard_map/transpose | solution.py:181
  (28 shorter events, 0.3 us)
Async XLA Ops:
  0.6 6.6 %copy-start.11 = (f32[8,3,1024]{2,0,1:T(8,128)S(1)}, f32[8,3,1024]{2,0,1:T(8,128)}, u32[]{:S(2)}) copy-start(f32[8,3,1024]{2,0,1:T(8,128)} %param.10) | copy-start | bytes 294916
  1.7 12.1 %collective-permute-start.1 = (bf16[2,256,384]{2,1,0:T(8,128)(2,1)S(1)}, bf16[2,256,384]{2,1,0:T(8,128)(2,1)S(1)}, u32[]{:S(2)}, u32[]{:S(2)}) collective-permute-start(bf16[2,256,384]{2,1,0:T(8,128)(2,1)S(1)} %slice.26.refs_0_), channel_id=1, source_target_pairs={{0,16},{8,24},{16,0},{24,8},{1,17},{9,25},{17,1},{25,9},{2,18},{10... | collective-permute-start | bytes 1179656 | tf_op jit(solution)/shard_map/ppermute | solution.py:17
  4.7 25.5 %collective-permute-start = (bf16[2,256,384]{2,1,0:T(8,128)(2,1)S(1)}, bf16[2,256,384]{2,1,0:T(8,128)(2,1)}, u32[]{:S(2)}, u32[]{:S(2)}) collective-permute-start(bf16[2,256,384]{2,1,0:T(8,128)(2,1)S(1)} %slice.26.refs_0_), channel_id=1, source_target_pairs={{0,8},{8,0},{16,24},{24,16},{1,9},{9,1},{17,25},{25,17},{2,10},{10... | collective-permute-start | bytes 1179656 | tf_op jit(solution)/shard_map/ppermute | solution.py:17
  7.2 11.3 %copy-start.12 = (f32[2,3,1024]{2,0,1:T(2,128)S(1)}, f32[2,3,1024]{2,0,1:T(2,128)}, u32[]{:S(2)}) copy-start(f32[2,3,1024]{2,0,1:T(2,128)} %param.7) | copy-start | bytes 73732
  13.9 7.1 %copy-start.4 = (bf16[2,256,384]{2,1,0:T(8,128)(2,1)}, bf16[2,256,384]{2,1,0:T(8,128)(2,1)S(1)}, u32[]{:S(2)}) copy-start(bf16[2,256,384]{2,1,0:T(8,128)(2,1)S(1)} %collective-permute-done.1.refs_2_) | copy-start | bytes 1179652
  13.9 28.5 %collective-permute-start.4 = (bf16[6,256,384]{2,1,0:T(8,128)(2,1)}, bf16[6,256,384]{2,1,0:T(8,128)(2,1)}, u32[]{:S(2)}, u32[]{:S(2)}) collective-permute-start(bf16[6,256,384]{2,1,0:T(8,128)(2,1)} %slice.30.refs_0_), channel_id=1, source_target_pairs={{0,16},{8,24},{16,0},{24,8},{1,17},{9,25},{17,1},{25,9},{2,18},{10... | collective-permute-start | bytes 3538952 | tf_op jit(solution)/shard_map/ppermute | solution.py:17
  15.6 14.6 %collective-permute-start.2 = (bf16[2,256,384]{2,1,0:T(8,128)(2,1)S(1)}, bf16[2,256,384]{2,1,0:T(8,128)(2,1)}, u32[]{:S(2)}, u32[]{:S(2)}) collective-permute-start(bf16[2,256,384]{2,1,0:T(8,128)(2,1)S(1)} %collective-permute-done.1.refs_2_), channel_id=1, source_target_pairs={{0,8},{8,0},{16,24},{24,16},{1,9},{9,1},{17,25},{25,17},{2,10},{10... | collective-permute-start | bytes 1179656 | tf_op jit(solution)/shard_map/ppermute | solution.py:17
  15.7 0.6 copy-start.9
  18.8 2.1 %copy-start.1 = (f32[2,3,1024]{1,2,0:T(8,128)}, f32[2,3,1024]{1,2,0:T(8,128)S(1)}, u32[]{:S(2)}) copy-start(f32[2,3,1024]{1,2,0:T(8,128)S(1)} %copy.15) | copy-start | bytes 73732
  21.0 9.3 %copy-start.3 = (bf16[2,384,512]{2,1,0:T(8,128)(2,1)S(1)}, bf16[2,384,512]{2,1,0:T(8,128)(2,1)}, u32[]{:S(2)}) copy-start(bf16[2,384,512]{2,1,0:T(8,128)(2,1)} %slice.27.refs_4_) | copy-start | bytes 2359300
  21.0 9.3 %copy-start.5 = (bf16[2,256,384]{2,1,0:T(8,128)(2,1)S(1)}, bf16[2,256,384]{2,1,0:T(8,128)(2,1)}, u32[]{:S(2)}) copy-start(bf16[2,256,384]{2,1,0:T(8,128)(2,1)} %copy-done.4) | copy-start | bytes 1179652
  21.0 9.3 %copy-start.6 = (s32[8]{0:T(128)S(1)}, s32[8]{0:T(128)}, u32[]{:S(2)}) copy-start(s32[8]{0:T(128)} %param.12) | copy-start | bytes 100
  21.0 9.3 %copy-start.7 = (s32[2]{0:T(128)S(1)}, s32[2]{0:T(128)}, u32[]{:S(2)}) copy-start(s32[2]{0:T(128)} %test_counts_ref.3) | copy-start | bytes 28
  35.2 1.0 copy-start
  36.2 6.5 %copy-start.10 = (f32[8,3,1024]{2,1,0:T(4,128)S(1)}, f32[8,3,1024]{2,1,0:T(4,128)}, u32[]{:S(2)}) copy-start(f32[8,3,1024]{2,1,0:T(4,128)} %copy-done.9) | copy-start | bytes 294916
  36.2 57.0 %all-to-all-start = ((bf16[8,2,2,48,384]{4,3,2,1,0:T(8,128)(2,1)}), bf16[8,2,2,48,384]{4,3,2,1,0:T(8,128)(2,1)}, u32[]{:S(2)}, u32[]{:S(2)}) async-start(bf16[8,2,2,48,384]{4,3,2,1,0:T(8,128)(2,1)} %copy-done), calls=%async_computation | async-start | bytes 2359296 | tf_op jit(solution)/shard_map/all_to_all | solution.py:180
  42.2 35.6 %collective-permute-start.3 = (bf16[6,256,384]{2,1,0:T(8,128)(2,1)}, bf16[6,256,384]{2,1,0:T(8,128)(2,1)S(1)}, u32[]{:S(2)}, u32[]{:S(2)}) collective-permute-start(bf16[6,256,384]{2,1,0:T(8,128)(2,1)} %slice.30.refs_0_), channel_id=1, source_target_pairs={{0,8},{8,0},{16,24},{24,16},{1,9},{9,1},{17,25},{25,17},{2,10},{10... | collective-permute-start | bytes 3538952 | tf_op jit(solution)/shard_map/ppermute | solution.py:17
  42.4 35.4 %collective-permute-start.5 = (bf16[6,256,384]{2,1,0:T(8,128)(2,1)}, bf16[6,256,384]{2,1,0:T(8,128)(2,1)S(1)}, u32[]{:S(2)}, u32[]{:S(2)}) collective-permute-start(bf16[6,256,384]{2,1,0:T(8,128)(2,1)} %collective-permute-done.4.refs_2_), channel_id=1, source_target_pairs={{0,8},{8,0},{16,24},{24,16},{1,9},{9,1},{17,25},{25,17},{2,10},{10... | collective-permute-start | bytes 3538952 | tf_op jit(solution)/shard_map/ppermute | solution.py:17
  42.8 1.9 copy-start.2
  74.1 3.7 %copy-start.8 = (bf16[2,6,384,1024]{3,2,1,0:T(8,128)(2,1)}, bf16[2,6,384,1024]{3,2,1,0:T(8,128)(2,1)S(1)}, u32[]{:S(2)}) copy-start(bf16[2,6,384,1024]{3,2,1,0:T(8,128)(2,1)S(1)} %shard_map.88.left_ref) | copy-start | bytes 28311556
  93.3 99.2 %all-to-all-start.1 = ((bf16[8,2,6,48,384]{4,3,2,1,0:T(8,128)(2,1)}), bf16[8,2,6,48,384]{4,3,2,1,0:T(8,128)(2,1)}, u32[]{:S(2)}, u32[]{:S(2)}) async-start(bf16[8,2,6,48,384]{4,3,2,1,0:T(8,128)(2,1)} %get-tuple-element.9), calls=%async_computation.1 | async-start | bytes 7077888 | tf_op jit(solution)/shard_map/all_to_all | solution.py:180
  99.8 37.8 %collective-permute-start.6 = (bf16[2,2,2,48,512]{4,3,2,1,0:T(8,128)(2,1)S(1)}, bf16[2,2,2,48,512]{4,3,2,1,0:T(8,128)(2,1)S(1)}, u32[]{:S(2)}, u32[]{:S(2)}) collective-permute-start(bf16[2,2,2,48,512]{4,3,2,1,0:T(8,128)(2,1)S(1)} %fusion), channel_id=1, source_target_pairs={{0,1},{1,0},{2,3},{3,2},{4,5},{5,4},{6,7},{7,6},{8,9},{9,8},{10,11... | collective-permute-start | bytes 1179656 | tf_op jit(solution)/shard_map/ppermute | solution.py:17
  137.8 49.2 %collective-permute-start.7 = (bf16[2,2,48,512]{3,2,1,0:T(8,128)(2,1)S(1)}, bf16[2,2,48,512]{3,2,1,0:T(8,128)(2,1)S(1)}, u32[]{:S(2)}, u32[]{:S(2)}) collective-permute-start(bf16[2,2,48,512]{3,2,1,0:T(8,128)(2,1)S(1)} %fusion.1), channel_id=1, source_target_pairs={{0,4},{1,5},{2,6},{3,7},{4,0},{5,1},{6,2},{7,3},{8,12},{9,13},{10,... | collective-permute-start | bytes 589832 | tf_op jit(solution)/shard_map/ppermute | solution.py:17
  187.1 4.7 %collective-permute-start.8 = (bf16[2,48,512]{2,1,0:T(8,128)(2,1)S(1)}, bf16[2,48,512]{2,1,0:T(8,128)(2,1)S(1)}, u32[]{:S(2)}, u32[]{:S(2)}) collective-permute-start(bf16[2,48,512]{2,1,0:T(8,128)(2,1)S(1)} %fusion.3), channel_id=1, source_target_pairs={{0,2},{1,3},{2,0},{3,1},{4,6},{5,7},{6,4},{7,5},{8,10},{9,11},{10,... | collective-permute-start | bytes 294920 | tf_op jit(solution)/shard_map/ppermute | solution.py:17
where the time goes:
time: 200 us; the launch traced here: 199 us
  waiting for transfers between devices  94.6 us (47%)
  Pallas kernels  59 us (30%)
  starting transfers between devices  21.1 us (11%)
  local copies, waits for them, and re-layouts  19.2 us (10%)
  other arithmetic  4.05 us (2%)
    ppermute x9, waiting for transfers between devices, exchange(): return lax.ppermute(x, axis, [(a, a ^ flip) for a in range(size)])  94.6 us
    pallas_call x2, Pallas kernels, left_products(): pl.pallas_call(left_kernel, grid=(ntest, nsource), out_shape=jax.ShapeDty...  38.5 us
    pallas_call x2, Pallas kernels, tiles_and_sums(): pl.pallas_call(functools.partial(tile_kernel, nshard, ndest), grid=(ntest...  20.4 us
    all_to_all x2, starting transfers between devices, body(): lax.all_to_all(tiles, 'src', split_axis=0, concat_axis=0, tiled=True)  11.9 us
    ppermute x9, starting transfers between devices, exchange(): return lax.ppermute(x, axis, [(a, a ^ flip) for a in range(size)])  9.11 us
    unnamed x31, local copies, waits for them, and re-layouts  7.88 us
  transfers between devices with their start and end apart: 11, of which 4 were waited for; matrix products, arithmetic and copies ran while one was open for 5% of the time, Pallas kernels for 30%

commit v1 on v0

v1 whole, which is shorter than its diff:
```python
import functools

import jax
import jax.numpy as jnp
from jax import lax
from jax.experimental import pallas as pl
from jax.experimental.pallas import tpu as pltpu
from jax.sharding import PartitionSpec as P

softening = 0.0025
QBLOCK = 256
VMEM_LIMIT = 40 * 1024 * 1024


def exchange(x, axis, flip):
    size = lax.axis_size(axis)
    return lax.ppermute(x, axis, [(a, a ^ flip) for a in range(size)])


def bits_down(size):
    bit = size // 2
    while bit >= 1:
        yield bit
        bit //= 2


def three_terms(x):
    high = lax.reduce_precision(x, 8, 7)
    middle = lax.reduce_precision(x - high, 8, 7)
    return high, middle, x - high - middle


def distance_features(points, is_test):
    centred = points - 0.5
    norm = jnp.sum(centred * centred, axis=1, keepdims=True)
    if is_test:
        norm = norm + softening
    terms = three_terms(centred)
    if is_test:
        cross = [-2.0 * a for a in terms for _ in range(3)]
    else:
        cross = [b for _ in range(3) for b in terms]
    ones = [jnp.ones_like(norm)] * 3
    norms = list(three_terms(norm))
    rows = cross + (norms + ones if is_test else ones + norms)
    features = jnp.concatenate(rows, axis=1).astype(jnp.bfloat16)
    pad = -features.shape[1] % 16
    return jnp.pad(features, ((0, 0), (0, pad), (0, 0)))


def left_kernel(test_ref, source_ref, basis_ref, out_ref):
    nq = source_ref.shape[2]
    block = min(QBLOCK, nq)

    def kernel_block(start):
        squared = jnp.dot(
            test_ref[0], source_ref[0, :, start : start + block], preferred_element_type=jnp.float32
        )
        return lax.rsqrt(squared.astype(jnp.bfloat16))

    ready = kernel_block(0)
    for start in range(0, nq, block):
        now = ready
        if start + block < nq:
            ready = kernel_block(start + block)
        out_ref[0, 0, :, start : start + block] = jnp.dot(
            basis_ref[0], now, preferred_element_type=jnp.float32
        ).astype(jnp.bfloat16)


def left_products(test_features, source_features, basis_rows, first, last):
    ntest, npoint, nfeature = test_features.shape
    nq = source_features.shape[2]
    kmax = basis_rows.shape[1]
    nsource = last - first
    return pl.pallas_call(
        left_kernel,
        grid=(ntest, nsource),
        out_shape=jax.ShapeDtypeStruct((ntest, nsource, kmax, nq), jnp.bfloat16),
        in_specs=[
            pl.BlockSpec((1, npoint, nfeature), lambda i, j: (i, 0, 0)),
            pl.BlockSpec((1, nfeature, nq), lambda i, j: (first + j, 0, 0)),
            pl.BlockSpec((1, kmax, npoint), lambda i, j: (i, 0, 0)),
        ],
        out_specs=pl.BlockSpec((1, 1, kmax, nq), lambda i, j: (i, j, 0, 0)),
        compiler_params=pltpu.CompilerParams(vmem_limit_bytes=VMEM_LIMIT),
        cost_estimate=pl.CostEstimate(
            flops=2 * ntest * nsource * npoint * nq * kmax,
            bytes_accessed=2 * ntest * nsource * kmax * nq,
            transcendentals=ntest * nsource * npoint * nq,
        ),
    )(test_features, source_features, basis_rows)


def tile_kernel(nshard, ndest, first, has_start, test_counts_ref, source_counts_ref, left_ref, *refs):
    shard_refs, coeff_ref = refs[:nshard], refs[nshard]
    start_ref = refs[nshard + 1] if has_start else None
    tile_ref, sum_ref, total_ref = refs[-3:]
    j, i = pl.program_id(0), pl.program_id(1)
    kmax = left_ref.shape[2]
    part = left_ref.shape[3] // nshard
    tile = None
    for place, shard_ref in enumerate(shard_refs):
        term = jnp.dot(
            left_ref[0, 0, :, place * part : (place + 1) * part],
            shard_ref[0],
            preferred_element_type=jnp.float32,
        )
        tile = term if tile is None else tile + term
    row_ids = lax.broadcasted_iota(jnp.int32, tile.shape, 0)
    column_ids = lax.broadcasted_iota(jnp.int32, tile.shape, 1)
    used = (row_ids < test_counts_ref[i]) & (column_ids < source_counts_ref[first + j])
    tile = jnp.where(used, tile, 0.0)
    rows = kmax // ndest
    for dest in range(ndest):
        tile_ref[dest, 0, 0] = tile[dest * rows : (dest + 1) * rows].astype(jnp.bfloat16)
    term = jnp.dot(tile.astype(jnp.bfloat16), coeff_ref[0], preferred_element_type=jnp.float32)

    @pl.when(j == 0)
    def _():
        total_ref[i] = term + start_ref[i] if has_start else term

    @pl.when(j > 0)
    def _():
        total_ref[i] += term

    @pl.when(j == pl.num_programs(0) - 1)
    def _():
        sum_ref[i] = total_ref[i].astype(sum_ref.dtype)


def tiles_and_sums(ndest, first, test_counts, source_counts, left, shards, coefficients, start):
    ntest, nsource, kmax, nq = left.shape
    nshard = len(shards)
    part, width = shards[0].shape[1:]
    ncol = coefficients.shape[2]
    rows = kmax // ndest
    smem = pl.BlockSpec(memory_space=pltpu.SMEM)
    whole_sum = pl.BlockSpec((ntest, kmax, ncol), lambda j, i: (0, 0, 0))
    has_start = start is not None
    sum_dtype = jnp.bfloat16 if has_start else jnp.float32
    return pl.pallas_call(
        functools.partial(tile_kernel, nshard, ndest, first, has_start),
        grid=(nsource, ntest),
        out_shape=(
            jax.ShapeDtypeStruct((ndest, ntest, nsource, rows, width), jnp.bfloat16),
            jax.ShapeDtypeStruct((ntest, kmax, ncol), sum_dtype),
        ),
        in_specs=[smem, smem, pl.BlockSpec((1, 1, kmax, nq), lambda j, i: (i, j, 0, 0))]
        + [pl.BlockSpec((1, part, width), lambda j, i: (j, 0, 0))] * nshard
        + [pl.BlockSpec((1, kmax, ncol), lambda j, i: (first + j, 0, 0))]
        + ([whole_sum] if has_start else []),
        out_specs=(
            pl.BlockSpec((ndest, 1, 1, rows, width), lambda j, i: (0, i, j, 0, 0)),
            whole_sum,
        ),
        scratch_shapes=[pltpu.VMEM((ntest, kmax, ncol), jnp.float32)],
        compiler_params=pltpu.CompilerParams(vmem_limit_bytes=VMEM_LIMIT),
        cost_estimate=pl.CostEstimate(
            flops=2 * ntest * nsource * kmax * width * (nq + ncol),
            bytes_accessed=2 * ntest * nsource * kmax * (nq + width),
            transcendentals=0,
        ),
    )(test_counts, source_counts, left, *shards, coefficients, *([start] if has_start else []))


def body(
    test_points, test_basis, test_counts, source_points, source_basis, source_counts, coefficients
):
    nsource, part, kmax = source_basis.shape
    ntest = test_points.shape[0]
    nsrc = lax.axis_size("src")
    ntest_axis = lax.axis_size("test")
    rows = kmax // nsrc
    me_test = lax.axis_index("test")
    points = jnp.concatenate(
        [
            lax.dynamic_slice_in_dim(source_points, (me_test ^ offset) * part, part, 2)
            for offset in range(ntest_axis)
        ],
        axis=2,
    )
    source_features = distance_features(points, False)
    test_features = distance_features(test_points, True).transpose(0, 2, 1)
    basis_rows = test_basis.transpose(0, 2, 1)
    cut = max(1, nsource // 4)
    held = {}

    def gather(name, shard, left):
        got = {0: shard}
        bits = list(bits_down(ntest_axis))
        for bit in bits:
            if bit == bits[-1] and left is not None:
                names = [o for o in got if o != 0]
                tied = lax.optimization_barrier(tuple(got[o] for o in names) + (left,))
                got.update(zip(names, tied[:-1]))
                left = tied[-1]
            for offset in list(got):
                got[offset ^ bit] = exchange(got[offset], "test", bit)
            if bit == bits[0]:
                held[name] = got[bit]
        return [got[offset] for offset in sorted(got)], left

    left_a = left_products(test_features, source_features, basis_rows, 0, cut)
    shards_a, left_a = gather("a", source_basis[:cut], left_a)
    tiles_a, sums_a = tiles_and_sums(
        nsrc, 0, test_counts, source_counts, left_a, shards_a, coefficients, None
    )
    moved_a = lax.all_to_all(tiles_a, "src", split_axis=0, concat_axis=0, tiled=True)

    rest, _ = lax.optimization_barrier((source_basis[cut:], held["a"]))
    features_b, _ = lax.optimization_barrier((source_features, tiles_a))
    left_b = left_products(test_features, features_b, basis_rows, cut, nsource)
    shards_b, left_b = gather("b", rest, left_b)
    tiles_b, summed = tiles_and_sums(
        nsrc, cut, test_counts, source_counts, left_b, shards_b, coefficients, sums_a
    )
    projected = lax.psum_scatter(summed, "src", scatter_dimension=1, tiled=True)
    moved_b = lax.all_to_all(tiles_b, "src", split_axis=0, concat_axis=0, tiled=True)

    reduced = jnp.concatenate([moved_a, moved_b], axis=2).transpose(1, 3, 0, 2, 4)
    reduced = reduced.reshape(ntest, rows, nsrc * nsource, kmax)
    return (reduced, projected)


def solution(mesh):
    return jax.shard_map(
        body,
        mesh=mesh,
        in_specs=(
            P("test", None, None),
            P("test", None, None),
            P("test"),
            P("src", None, None),
            P("src", "test", None),
            P("src"),
            P("src", None, None),
        ),
        out_specs=(P("test", "src", None, None), P("test", "src", None)),
        check_vma=False,
    )
```

time: 200 us -> 214 us (1.070)
  between operations: 0.93 us -> 14.3 us
  Pallas kernels: 59 us -> 46.9 us
  waiting for transfers between devices: 94.6 us -> 104 us
  other arithmetic: 4.05 us -> 10.8 us
  starting transfers between devices: 21.1 us -> 15.7 us
    ppermute x9 -> x6, waiting for transfers between devices: 94.6 us -> 3.18 us  [exchange(): return lax.ppermute(x, axis, [(a, a ^ flip) for a in range(size)])]
    all_to_all x2, waiting for transfers between devices: 0.01 us -> 85.2 us  [the longest x1 85.2 us: body(): lax.all_to_all(tiles_b, 'src', split_axis=0, concat_axis=0, tiled=True)]
    reduce_scatter x0 -> x1, waiting for transfers between devices: none -> 15.1 us  [body(): projected = lax.psum_scatter(summed, 'src', scatter_dimension=1, tiled=True)]
    pallas_call x2, Pallas kernels: 38.5 us -> 25.8 us  [left_products(): pl.pallas_call(left_kernel, grid=(ntest, nsource), out_shape=jax.ShapeDty...]
    unnamed x0 -> x12, other arithmetic: none -> 6.94 us
    slice x7 -> x2, local copies, waits for them, and re-layouts: 7.58 us -> 2.3 us  [the longest x1 1.16 us: body(): shards_a, left_a = gather('a', source_basis[:cut], left_a)]
    ppermute x9 -> x6, starting transfers between devices: 9.11 us -> 3.85 us  [exchange(): return lax.ppermute(x, axis, [(a, a ^ flip) for a in range(size)])]
    unnamed x31 -> x35, local copies, waits for them, and re-layouts: 7.88 us -> 12.9 us
  transfers between devices with their start and end apart: 11 -> 9, of which waited for: 4 -> 4; matrix products, arithmetic and copies ran while one was open for 5% -> 9% of each run, Pallas kernels for 30% -> 22%
where the time goes in v1:
time: 214 us; the launch traced here: 213 us
  waiting for transfers between devices  104 us (49%)
  Pallas kernels  46.9 us (22%)
  local copies, waits for them, and re-layouts  21.2 us (10%)
  starting transfers between devices  15.7 us (7%)
  between operations  14.3 us (7%)
  other arithmetic  10.8 us (5%)
    all_to_all x1, waiting for transfers between devices, body(): lax.all_to_all(tiles_b, 'src', split_axis=0, concat_axis=0, tiled=True)  85.2 us
    pallas_call x2, Pallas kernels, left_products(): pl.pallas_call(left_kernel, grid=(ntest, nsource), out_shape=jax.ShapeDty...  25.8 us
    pallas_call x2, Pallas kernels, tiles_and_sums(): pl.pallas_call(functools.partial(tile_kernel, nshard, ndest, first, has_s...  21.1 us
    reduce_scatter x1, waiting for transfers between devices, body(): projected = lax.psum_scatter(summed, 'src', scatter_dimension=1, tiled=True)  15.1 us
    unnamed x35, local copies, waits for them, and re-layouts  12.9 us
    unnamed x12, other arithmetic  6.94 us
    all_to_all x1, starting transfers between devices, body(): lax.all_to_all(tiles_b, 'src', split_axis=0, concat_axis=0, tiled=True)  6.02 us
    all_to_all x1, starting transfers between devices, body(): lax.all_to_all(tiles_a, 'src', split_axis=0, concat_axis=0, tiled=True)  5.81 us
  transfers between devices with their start and end apart: 9, of which 4 were waited for; matrix products, arithmetic and copies ran while one was open for 9% of the time, Pallas kernels for 22%

profile of v1, /device:TPU:0, one launch (start us, length us, event | category | flops | bytes accessed | tf_op | source)
XLA Modules:
  0.0 213.0 jit_solution(16502595725328380356)
XLA Ops:
  7.2 1.2 slice.6.refs_0_
  8.3 0.5 collective-permute-start.1
  8.8 2.6 %collective-permute-start = (bf16[2,256,384]{2,1,0:T(8,128)(2,1)S(1)}, bf16[2,256,384]{2,1,0:T(8,128)(2,1)}, u32[]{:S(2)}, u32[]{:S(2)}) collective-permute-start(bf16[2,256,384]{2,1,0:T(8,128)(2,1)S(1)} %slice.6.refs_0_), channel_id=1, source_target_pairs={{0,16},{8,24},{16,0},{24,8},{1,17},{9,25},{17,1},{25,9},{2,18},{10... | collective-permute-start | bytes 1179656 | tf_op jit(solution)/shard_map/ppermute | solution.py:17
  11.4 0.8 multiply_reduce_fusion.1
  12.2 0.8 constant_dynamic-update-slice_fusion.12
  13.0 0.8 constant_dynamic-slice_fusion.3
  13.9 0.2 multiply_reduce_fusion
  14.1 0.1 fusion.1
  14.1 0.8 constant_dynamic-update-slice_fusion.11
  14.9 0.8 constant_dynamic-update-slice_fusion.10
  15.7 0.8 constant_dynamic-update-slice_fusion.9
  16.4 0.8 constant_dynamic-update-slice_fusion.8
  17.2 0.8 constant_dynamic-update-slice_fusion.7
  18.0 0.8 constant_dynamic-update-slice_fusion.6
  18.7 0.8 constant_dynamic-update-slice_fusion.5
  19.5 0.8 constant_dynamic-update-slice_fusion.4
  20.3 0.3 copy.35
  20.7 1.6 copy.41
  22.3 1.2 concatenate.24
  23.5 0.1 pad.9.source_ref
  23.6 0.1 pad_bitcast_fusion.test_ref
  23.8 0.0 copy-start.1
  23.8 1.8 copy-done.1
  25.5 6.5 %shard_map.86.left_ref = bf16[2,2,384,1024]{3,2,1,0:T(8,128)(2,1)S(1)} custom-call(bf16[2,1024,48]{2,1,0:T(8,128)(2,1)S(1)} %pad_bitcast_fusion.test_ref, bf16[8,48,1024]{2,1,0:T(8,128)(2,1)S(1)} %pad.9.source_ref, bf16[2,384,1024]{2,1,0:T(8,128)(2,1)S(1)} %bitcast.17), custom_call_target="tpu_custom_call" | custom-call | flops 3221225472 | bytes 3145728 | tf_op jit(solution)/shard_map/pallas_call | solution.py:76
  32.0 0.2 collective-permute-start.2
  32.3 1.1 slice.7.refs_0_
  33.4 0.3 collective-permute-start.3
  33.7 0.1 collective-permute-start.4
  33.8 0.3 collective-permute-done.2.refs_3_
  34.0 5.0 %shard_map.87 = (bf16[8,2,2,48,384]{4,3,2,1,0:T(8,128)(2,1)S(1)}, f32[2,384,512]{2,1,0:T(8,128)S(1)}) custom-call(s32[2]{0:T(128)S(1)} %copy-done.8, s32[8]{0:T(128)S(1)} %copy-done.9, bf16[2,2,384,1024]{3,2,1,0:T(8,128)(2,1)S(1)} %shard_map.86.left_ref, bf16[2,256,384]{2,1,0:T(8,128)(2,1)S(1)} %slice.6.refs_0_, ...), custom_call_target="tpu_custom_call" | custom-call | flops 1811939328 | bytes 4325376 | tf_op jit(solution)/shard_map/pallas_call | solution.py:142
  39.1 1.0 copy-done.3
  40.1 1.1 copy-done.10
  41.3 5.8 %all-to-all-start = ((bf16[8,2,2,48,384]{4,3,2,1,0:T(8,128)(2,1)}), bf16[8,2,2,48,384]{4,3,2,1,0:T(8,128)(2,1)}, u32[]{:S(2)}, u32[]{:S(2)}) async-start(bf16[8,2,2,48,384]{4,3,2,1,0:T(8,128)(2,1)} %copy-done.3), calls=%async_computation | async-start | bytes 2359296 | tf_op jit(solution)/shard_map/all_to_all | solution.py:209
  47.1 1.4 copy-done.2
  48.5 1.1 copy-done.5
  49.6 1.0 copy-done.7
  50.7 19.3 %shard_map.88.left_ref = bf16[2,6,384,1024]{3,2,1,0:T(8,128)(2,1)S(1)} custom-call(bf16[2,1024,48]{2,1,0:T(8,128)(2,1)S(1)} %copy-done.7, bf16[8,48,1024]{2,1,0:T(8,128)(2,1)S(1)} %copy-done.5, bf16[2,384,1024]{2,1,0:T(8,128)(2,1)S(1)} %bitcast.18), custom_call_target="tpu_custom_call" | custom-call | flops 9663676416 | bytes 9437184 | tf_op jit(solution)/shard_map/pallas_call | solution.py:76
  70.0 3.7 %copy-done.12 = bf16[2,6,384,1024]{3,2,1,0:T(8,128)(2,1)} copy-done((bf16[2,6,384,1024]{3,2,1,0:T(8,128)(2,1)}, bf16[2,6,384,1024]{3,2,1,0:T(8,128)(2,1)S(1)}, u32[]{:S(2)}) %copy-start.12) | copy-done | bytes 9437208
  73.6 0.2 collective-permute-start.5
  73.8 2.9 %collective-permute-done.5.refs_3_ = bf16[6,256,384]{2,1,0:T(8,128)(2,1)S(1)} collective-permute-done((bf16[6,256,384]{2,1,0:T(8,128)(2,1)}, bf16[6,256,384]{2,1,0:T(8,128)(2,1)S(1)}, u32[]{:S(2)}, u32[]{:S(2)}) %collective-permute-start.5) | collective-permute-done | bytes 1179680 | tf_op jit(solution)/shard_map/ppermute | solution.py:17
  76.7 16.1 %shard_map.89 = (bf16[8,2,6,48,384]{4,3,2,1,0:T(8,128)(2,1)}, bf16[2,384,512]{2,1,0:T(8,128)(2,1)}) custom-call(s32[2]{0:T(128)S(1)} %copy-done.8, s32[8]{0:T(128)S(1)} %copy-done.9, bf16[2,6,384,1024]{3,2,1,0:T(8,128)(2,1)} %copy-done.12, bf16[6,256,384]{2,1,0:T(8,128)(2,1)} %slice.7.refs_0_, bf16[6,256,384]{2,1,0:T(8,128)(2,1)} %collective-permute-done.4.refs_1_, ...), custom_call_target="tpu_custom_call" | custom-call | flops 5435817984 | bytes 12976128 | tf_op jit(solution)/shard_map/pallas_call | solution.py:142
  92.8 6.0 %all-to-all-start.1 = ((bf16[8,2,6,48,384]{4,3,2,1,0:T(8,128)(2,1)}), bf16[8,2,6,48,384]{4,3,2,1,0:T(8,128)(2,1)}, u32[]{:S(2)}, u32[]{:S(2)}) async-start(bf16[8,2,6,48,384]{4,3,2,1,0:T(8,128)(2,1)} %get-tuple-element.20), calls=%async_computation.1 | async-start | bytes 7077888 | tf_op jit(solution)/shard_map/all_to_all | solution.py:219
  98.8 0.0 reduce-scatter.2.cloned.1.call-start
  98.9 0.7 reduce-scatter.2.cloned.1.call-update
  99.5 85.2 %all-to-all-done.1 = bf16[8,2,6,48,384]{4,3,2,1,0:T(8,128)(2,1)} async-done(((bf16[8,2,6,48,384]{4,3,2,1,0:T(8,128)(2,1)}), bf16[8,2,6,48,384]{4,3,2,1,0:T(8,128)(2,1)}, u32[]{:S(2)}, u32[]{:S(2)}) %all-to-all-start.1) | async-done | bytes 3538976 | tf_op jit(solution)/shard_map/all_to_all | solution.py:219
  184.7 2.9 %maximum_bitcast_fusion = bf16[2,48,8,8,384]{4,1,3,0,2:T(8,128)(2,1)S(1)} fusion(bf16[8,2,6,48,384]{4,3,2,1,0:T(8,128)(2,1)} %all-to-all-done.1, bf16[8,2,2,48,384]{4,3,2,1,0:T(8,128)(2,1)} %all-to-all-done), kind=kLoop, calls=%fused_computation | loop fusion | flops 2359296 | bytes 9437184 | tf_op jit(solution)/shard_map/transpose | solution.py:221
  187.6 3.4 %copy.48 = bf16[2,48,8,8,384]{4,3,2,1,0:T(8,128)(2,1)} copy(bf16[2,48,8,8,384]{4,1,3,0,2:T(8,128)(2,1)S(1)} %maximum_bitcast_fusion) | data formatting | bytes 9437184 | tf_op jit(solution)/shard_map/transpose | solution.py:221
  191.0 15.1 %reduce-scatter.2.cloned.1.call-done = bf16[2,48,512]{2,1,0:T(8,128)(2,1)} async-done(((bf16[2,384,512]{2,1,0:T(8,128)(2,1)}), bf16[2,48,512]{2,1,0:T(8,128)(2,1)}) %reduce-scatter.2.cloned.1.call-update) | async-done | bytes 98320 | tf_op jit(solution)/shard_map/reduce_scatter | solution.py:218
  (36 shorter events, 0.2 us)
Async XLA Ops:
  7.2 13.5 %copy-start.13 = (bf16[2,1024,384]{2,1,0:T(8,128)(2,1)S(1)}, bf16[2,1024,384]{2,1,0:T(8,128)(2,1)}, u32[]{:S(2)}) copy-start(bf16[2,1024,384]{2,1,0:T(8,128)(2,1)} %param.8) | copy-start | bytes 4718596
  8.3 25.4 %collective-permute-start.1 = (bf16[2,256,384]{2,1,0:T(8,128)(2,1)S(1)}, bf16[2,256,384]{2,1,0:T(8,128)(2,1)}, u32[]{:S(2)}, u32[]{:S(2)}) collective-permute-start(bf16[2,256,384]{2,1,0:T(8,128)(2,1)S(1)} %slice.6.refs_0_), channel_id=1, source_target_pairs={{0,8},{8,0},{16,24},{24,16},{1,9},{9,1},{17,25},{25,17},{2,10},{10... | collective-permute-start | bytes 1179656 | tf_op jit(solution)/shard_map/ppermute | solution.py:17
  8.8 23.2 %collective-permute-start = (bf16[2,256,384]{2,1,0:T(8,128)(2,1)S(1)}, bf16[2,256,384]{2,1,0:T(8,128)(2,1)}, u32[]{:S(2)}, u32[]{:S(2)}) collective-permute-start(bf16[2,256,384]{2,1,0:T(8,128)(2,1)S(1)} %slice.6.refs_0_), channel_id=1, source_target_pairs={{0,16},{8,24},{16,0},{24,8},{1,17},{9,25},{17,1},{25,9},{2,18},{10... | collective-permute-start | bytes 1179656 | tf_op jit(solution)/shard_map/ppermute | solution.py:17
  23.6 8.4 %copy-start.4 = (bf16[8,48,1024]{2,1,0:T(8,128)(2,1)}, bf16[8,48,1024]{2,1,0:T(8,128)(2,1)S(1)}, u32[]{:S(2)}) copy-start(bf16[8,48,1024]{2,1,0:T(8,128)(2,1)S(1)} %pad.9.source_ref) | copy-start | bytes 2359300
  23.7 8.3 %copy-start.6 = (bf16[2,1024,48]{2,1,0:T(8,128)(2,1)}, bf16[2,1024,48]{2,1,0:T(8,128)(2,1)S(1)}, u32[]{:S(2)}) copy-start(bf16[2,1024,48]{2,1,0:T(8,128)(2,1)S(1)} %pad_bitcast_fusion.test_ref) | copy-start | bytes 589828
  23.8 1.8 copy-start.1
  25.5 6.7 %copy-start.14 = (bf16[8,256,384]{2,1,0:T(8,128)(2,1)S(1)}, bf16[8,256,384]{2,1,0:T(8,128)(2,1)}, u32[]{:S(2)}) copy-start(bf16[8,256,384]{2,1,0:T(8,128)(2,1)} %param.11) | copy-start | bytes 4718596
  25.5 8.5 %copy-start = (bf16[8,384,512]{2,1,0:T(8,128)(2,1)S(1)}, bf16[8,384,512]{2,1,0:T(8,128)(2,1)}, u32[]{:S(2)}) copy-start(bf16[8,384,512]{2,1,0:T(8,128)(2,1)} %refs_4_.3) | copy-start | bytes 9437188
  25.5 8.5 %copy-start.8 = (s32[2]{0:T(128)S(1)}, s32[2]{0:T(128)}, u32[]{:S(2)}) copy-start(s32[2]{0:T(128)} %test_counts_ref.3) | copy-start | bytes 28
  25.5 8.5 %copy-start.9 = (s32[8]{0:T(128)S(1)}, s32[8]{0:T(128)}, u32[]{:S(2)}) copy-start(s32[8]{0:T(128)} %source_counts_ref.3) | copy-start | bytes 100
  32.0 2.0 collective-permute-start.2
  33.4 40.2 %collective-permute-start.3 = (bf16[6,256,384]{2,1,0:T(8,128)(2,1)}, bf16[6,256,384]{2,1,0:T(8,128)(2,1)}, u32[]{:S(2)}, u32[]{:S(2)}) collective-permute-start(bf16[6,256,384]{2,1,0:T(8,128)(2,1)} %slice.7.refs_0_), channel_id=1, source_target_pairs={{0,16},{8,24},{16,0},{24,8},{1,17},{9,25},{17,1},{25,9},{2,18},{10... | collective-permute-start | bytes 3538952 | tf_op jit(solution)/shard_map/ppermute | solution.py:17
  33.7 40.1 %collective-permute-start.4 = (bf16[6,256,384]{2,1,0:T(8,128)(2,1)}, bf16[6,256,384]{2,1,0:T(8,128)(2,1)}, u32[]{:S(2)}, u32[]{:S(2)}) collective-permute-start(bf16[6,256,384]{2,1,0:T(8,128)(2,1)} %slice.7.refs_0_), channel_id=1, source_target_pairs={{0,8},{8,0},{16,24},{24,16},{1,9},{9,1},{17,25},{25,17},{2,10},{10... | collective-permute-start | bytes 3538952 | tf_op jit(solution)/shard_map/ppermute | solution.py:17
  39.1 1.0 copy-start.3
  40.1 1.1 copy-start.10
  41.3 51.5 %all-to-all-start = ((bf16[8,2,2,48,384]{4,3,2,1,0:T(8,128)(2,1)}), bf16[8,2,2,48,384]{4,3,2,1,0:T(8,128)(2,1)}, u32[]{:S(2)}, u32[]{:S(2)}) async-start(bf16[8,2,2,48,384]{4,3,2,1,0:T(8,128)(2,1)} %copy-done.3), calls=%async_computation | async-start | bytes 2359296 | tf_op jit(solution)/shard_map/all_to_all | solution.py:209
  47.1 1.4 copy-start.2
  48.5 1.1 copy-start.5
  49.6 1.0 copy-start.7
  50.6 26.1 %copy-start.11 = (f32[2,384,512]{2,1,0:T(8,128)S(1)}, f32[2,384,512]{2,1,0:T(8,128)}, u32[]{:S(2)}) copy-start(f32[2,384,512]{2,1,0:T(8,128)} %copy-done.10) | copy-start | bytes 4718596
  70.0 3.7 %copy-start.12 = (bf16[2,6,384,1024]{3,2,1,0:T(8,128)(2,1)}, bf16[2,6,384,1024]{3,2,1,0:T(8,128)(2,1)S(1)}, u32[]{:S(2)}) copy-start(bf16[2,6,384,1024]{3,2,1,0:T(8,128)(2,1)S(1)} %shard_map.88.left_ref) | copy-start | bytes 28311556
  73.6 3.1 %collective-permute-start.5 = (bf16[6,256,384]{2,1,0:T(8,128)(2,1)}, bf16[6,256,384]{2,1,0:T(8,128)(2,1)S(1)}, u32[]{:S(2)}, u32[]{:S(2)}) collective-permute-start(bf16[6,256,384]{2,1,0:T(8,128)(2,1)} %collective-permute-done.3.refs_2_), channel_id=1, source_target_pairs={{0,8},{8,0},{16,24},{24,16},{1,9},{9,1},{17,25},{25,17},{2,10},{10... | collective-permute-start | bytes 3538952 | tf_op jit(solution)/shard_map/ppermute | solution.py:17
  92.8 91.9 %all-to-all-start.1 = ((bf16[8,2,6,48,384]{4,3,2,1,0:T(8,128)(2,1)}), bf16[8,2,6,48,384]{4,3,2,1,0:T(8,128)(2,1)}, u32[]{:S(2)}, u32[]{:S(2)}) async-start(bf16[8,2,6,48,384]{4,3,2,1,0:T(8,128)(2,1)} %get-tuple-element.20), calls=%async_computation.1 | async-start | bytes 7077888 | tf_op jit(solution)/shard_map/all_to_all | solution.py:219
  98.8 107.3 %reduce-scatter.2.cloned.1.call-start = ((), (), s32[]{:S(2)}) async-start(), calls=%async_computation.3 | async-start | bytes 884736 | tf_op jit(solution)/shard_map/reduce_scatter | solution.py:218
Sparse Core Ops, SparseCore 0:
  103.5 102.5 reduce-scatter.1

commit v2 on v1

v2 whole, which is shorter than its diff:
```python
import functools

import jax
import jax.numpy as jnp
from jax import lax
from jax.experimental import pallas as pl
from jax.experimental.pallas import tpu as pltpu
from jax.sharding import PartitionSpec as P

softening = 0.0025
QBLOCK = 256
VMEM_LIMIT = 60 * 1024 * 1024


def exchange(x, axis, flip):
    size = lax.axis_size(axis)
    return lax.ppermute(x, axis, [(a, a ^ flip) for a in range(size)])


def bits_down(size):
    bit = size // 2
    while bit >= 1:
        yield bit
        bit //= 2


def sum_rows(total, axis):
    size = lax.axis_size(axis)
    me = lax.axis_index(axis)
    held, bit = total, 1
    while held.shape[0] > 4:
        pairs = held.reshape((held.shape[0] // 2, 2) + held.shape[1:])
        mine = (me // bit) % 2
        keep = lax.dynamic_index_in_dim(pairs, mine, 1, keepdims=False)
        give = lax.dynamic_index_in_dim(pairs, 1 - mine, 1, keepdims=False)
        got = exchange(give, axis, bit)
        held = (keep.astype(jnp.float32) + got.astype(jnp.float32)).astype(held.dtype)
        bit *= 2
    mine = me // bit
    result = lax.dynamic_index_in_dim(held, mine, 0, keepdims=False).astype(jnp.float32)
    for flip in range(1, held.shape[0]):
        give = lax.dynamic_index_in_dim(held, mine ^ flip, 0, keepdims=False)
        result = result + exchange(give, axis, flip * bit).astype(jnp.float32)
    return result.astype(total.dtype)


def features_kernel(test_ref, source_ref, test_out_ref, source_out_ref, rows_ref):
    def three_terms(x):
        high = x.astype(jnp.bfloat16).astype(jnp.float32)
        middle = (x - high).astype(jnp.bfloat16).astype(jnp.float32)
        return high, middle, x - high - middle

    def fill(centred, is_test):
        norm = jnp.sum(centred * centred, axis=0, keepdims=True)
        terms = three_terms(centred)
        norms = three_terms(norm + softening if is_test else norm)
        for a in range(3):
            for b in range(3):
                place = 3 * (3 * a + b)
                rows_ref[place : place + 3, :] = -2.0 * terms[a] if is_test else terms[b]
        for a in range(3):
            rows_ref[27 + a : 28 + a, :] = norms[a] if is_test else jnp.ones_like(norm)
            rows_ref[30 + a : 31 + a, :] = jnp.ones_like(norm) if is_test else norms[a]
        return rows_ref[...]

    rows_ref[...] = jnp.zeros_like(rows_ref)
    for i in range(test_ref.shape[0]):
        rows = fill(test_ref[i] - 0.5, True)
        test_out_ref[i] = rows.T.astype(jnp.bfloat16)
    for j in range(source_ref.shape[0]):
        rows = fill(source_ref[j] - 0.5, False)
        source_out_ref[j] = rows.astype(jnp.bfloat16)


NFEATURE = 128


def distance_features(test_points, source_points):
    ntest, _, npoint = test_points.shape
    nsource, _, nq = source_points.shape
    vmem = pl.BlockSpec(memory_space=pltpu.VMEM)
    return pl.pallas_call(
        features_kernel,
        out_shape=(
            jax.ShapeDtypeStruct((ntest, npoint, NFEATURE), jnp.bfloat16),
            jax.ShapeDtypeStruct((nsource, NFEATURE, nq), jnp.bfloat16),
        ),
        in_specs=[vmem, vmem],
        out_specs=(vmem, vmem),
        scratch_shapes=[pltpu.VMEM((NFEATURE, max(npoint, nq)), jnp.float32)],
        compiler_params=pltpu.CompilerParams(vmem_limit_bytes=VMEM_LIMIT),
    )(test_points, source_points)


def left_kernel(test_ref, source_ref, basis_ref, out_ref):
    nq = source_ref.shape[2]
    block = min(QBLOCK, nq)
    steps = [(i, start) for i in range(test_ref.shape[0]) for start in range(0, nq, block)]

    def kernel_block(i, start):
        squared = jnp.dot(
            test_ref[i], source_ref[0, :, start : start + block], preferred_element_type=jnp.float32
        )
        return lax.rsqrt(squared.astype(jnp.bfloat16))

    ready = kernel_block(*steps[0])
    for place, (i, start) in enumerate(steps):
        now = ready
        if place + 1 < len(steps):
            ready = kernel_block(*steps[place + 1])
        out_ref[i, 0, :, start : start + block] = jnp.dot(
            basis_ref[i], now, preferred_element_type=jnp.float32
        ).astype(jnp.bfloat16)


def left_products(test_features, source_features, basis_rows, first, last):
    ntest, npoint, nfeature = test_features.shape
    nq = source_features.shape[2]
    kmax = basis_rows.shape[1]
    nsource = last - first
    return pl.pallas_call(
        left_kernel,
        grid=(nsource,),
        out_shape=jax.ShapeDtypeStruct((ntest, nsource, kmax, nq), jnp.bfloat16),
        in_specs=[
            pl.BlockSpec((ntest, npoint, nfeature), lambda j: (0, 0, 0)),
            pl.BlockSpec((1, nfeature, nq), lambda j: (first + j, 0, 0)),
            pl.BlockSpec((ntest, kmax, npoint), lambda j: (0, 0, 0)),
        ],
        out_specs=pl.BlockSpec((ntest, 1, kmax, nq), lambda j: (0, j, 0, 0)),
        compiler_params=pltpu.CompilerParams(vmem_limit_bytes=VMEM_LIMIT),
        cost_estimate=pl.CostEstimate(
            flops=2 * ntest * nsource * npoint * nq * kmax,
            bytes_accessed=2 * ntest * nsource * kmax * nq,
            transcendentals=ntest * nsource * npoint * nq,
        ),
    )(test_features, source_features, basis_rows)


def tile_kernel(nshard, first, has_start, test_counts_ref, source_counts_ref, left_ref, *refs):
    shard_refs, coeff_ref = refs[:nshard], refs[nshard]
    start_ref = refs[nshard + 1] if has_start else None
    tile_ref, sum_ref, total_ref = refs[-3:]
    j = pl.program_id(0)
    ntest, _, kmax, nq = left_ref.shape
    ndest, _, _, rows, width = tile_ref.shape
    side = jnp.concatenate([shard_ref[0] for shard_ref in shard_refs], axis=0)
    row_ids = lax.broadcasted_iota(jnp.int32, (kmax, width), 0)
    column_ids = lax.broadcasted_iota(jnp.int32, (kmax, width), 1)
    tiles = jnp.dot(
        left_ref[...].reshape(ntest * kmax, nq), side, preferred_element_type=jnp.float32
    )
    masked = []
    for i in range(ntest):
        used = (row_ids < test_counts_ref[i]) & (column_ids < source_counts_ref[first + j])
        tile = jnp.where(used, tiles[i * kmax : (i + 1) * kmax], 0.0)
        for dest in range(ndest):
            tile_ref[dest, i, 0] = tile[dest * rows : (dest + 1) * rows].astype(jnp.bfloat16)
        masked.append(tile.astype(jnp.bfloat16))
    term = jnp.dot(jnp.concatenate(masked, axis=0), coeff_ref[0], preferred_element_type=jnp.float32)

    @pl.when(j == 0)
    def _():
        total_ref[...] = term + start_ref[...] if has_start else term

    @pl.when(j > 0)
    def _():
        total_ref[...] += term

    @pl.when(j == pl.num_programs(0) - 1)
    def _():
        if has_start:
            for i in range(ntest):
                for dest in range(ndest):
                    top = i * kmax + dest * rows
                    sum_ref[dest, i] = total_ref[top : top + rows, :].astype(sum_ref.dtype)
        else:
            sum_ref[...] = total_ref[...]


def tiles_and_sums(ndest, first, test_counts, source_counts, left, shards, coefficients, start):
    ntest, nsource, kmax, nq = left.shape
    nshard = len(shards)
    part, width = shards[0].shape[1:]
    ncol = coefficients.shape[2]
    rows = kmax // ndest
    smem = pl.BlockSpec(memory_space=pltpu.SMEM)
    total_spec = pl.BlockSpec((ntest * kmax, ncol), lambda j: (0, 0))
    has_start = start is not None
    if has_start:
        sum_shape = jax.ShapeDtypeStruct((ndest, ntest, rows, ncol), jnp.bfloat16)
        sum_spec = pl.BlockSpec((ndest, ntest, rows, ncol), lambda j: (0, 0, 0, 0))
    else:
        sum_shape = jax.ShapeDtypeStruct((ntest * kmax, ncol), jnp.float32)
        sum_spec = total_spec
    return pl.pallas_call(
        functools.partial(tile_kernel, nshard, first, has_start),
        grid=(nsource,),
        out_shape=(
            jax.ShapeDtypeStruct((ndest, ntest, nsource, rows, width), jnp.bfloat16),
            sum_shape,
        ),
        in_specs=[smem, smem, pl.BlockSpec((ntest, 1, kmax, nq), lambda j: (0, j, 0, 0))]
        + [pl.BlockSpec((1, part, width), lambda j: (j, 0, 0))] * nshard
        + [pl.BlockSpec((1, kmax, ncol), lambda j: (first + j, 0, 0))]
        + ([total_spec] if has_start else []),
        out_specs=(
            pl.BlockSpec((ndest, ntest, 1, rows, width), lambda j: (0, 0, j, 0, 0)),
            sum_spec,
        ),
        scratch_shapes=[pltpu.VMEM((ntest * kmax, ncol), jnp.float32)],
        compiler_params=pltpu.CompilerParams(vmem_limit_bytes=VMEM_LIMIT),
        cost_estimate=pl.CostEstimate(
            flops=2 * ntest * nsource * kmax * width * (nq + ncol),
            bytes_accessed=2 * ntest * nsource * kmax * (nq + width),
            transcendentals=0,
        ),
    )(test_counts, source_counts, left, *shards, coefficients, *([start] if has_start else []))


def body(
    test_points, test_basis, test_counts, source_points, source_basis, source_counts, coefficients
):
    nsource, part, kmax = source_basis.shape
    ntest = test_points.shape[0]
    nsrc = lax.axis_size("src")
    ntest_axis = lax.axis_size("test")
    rows = kmax // nsrc
    me_test = lax.axis_index("test")
    cut = max(1, nsource // 4)
    held = {}

    def gather(name, shard, left):
        got = {0: shard}
        bits = list(bits_down(ntest_axis))
        for bit in bits:
            if bit == bits[-1]:
                names = [o for o in got if o != 0]
                tied = lax.optimization_barrier(tuple(got[o] for o in names) + (left,))
                got.update(zip(names, tied[:-1]))
                left = tied[-1]
            for offset in list(got):
                got[offset ^ bit] = exchange(got[offset], "test", bit)
            if bit == bits[0]:
                held[name] = got[bit]
        return [got[offset] for offset in sorted(got)], left

    points = jnp.concatenate(
        [
            lax.dynamic_slice_in_dim(source_points, (me_test ^ offset) * part, part, 2)
            for offset in range(ntest_axis)
        ],
        axis=2,
    )
    test_features, source_features = distance_features(test_points, points)
    basis_rows = test_basis.transpose(0, 2, 1)

    left_a = left_products(test_features, source_features, basis_rows, 0, cut)
    shards_a, left_a = gather("a", source_basis[:cut], left_a)
    tiles_a, sums_a = tiles_and_sums(
        nsrc, 0, test_counts, source_counts, left_a, shards_a, coefficients, None
    )
    moved_a = lax.all_to_all(tiles_a, "src", split_axis=0, concat_axis=0, tiled=True)

    rest, _ = lax.optimization_barrier((source_basis[cut:], held["a"]))
    features_b, _ = lax.optimization_barrier((source_features, tiles_a))
    left_b = left_products(test_features, features_b, basis_rows, cut, nsource)
    shards_b, left_b = gather("b", rest, left_b)
    tiles_b, summed = tiles_and_sums(
        nsrc, cut, test_counts, source_counts, left_b, shards_b, coefficients, sums_a
    )
    projected = sum_rows(summed, "src")
    moved_b = lax.all_to_all(tiles_b, "src", split_axis=0, concat_axis=0, tiled=True)

    reduced = jnp.concatenate([moved_a, moved_b], axis=2).transpose(1, 3, 0, 2, 4)
    reduced = reduced.reshape(ntest, rows, nsrc * nsource, kmax)
    return (reduced, projected)


def solution(mesh):
    return jax.shard_map(
        body,
        mesh=mesh,
        in_specs=(
            P("test", None, None),
            P("test", None, None),
            P("test"),
            P("src", None, None),
            P("src", "test", None),
            P("src"),
            P("src", None, None),
        ),
        out_specs=(P("test", "src", None, None), P("test", "src", None)),
        check_vma=False,
    )
```

time: 214 us -> 177 us (0.83)
  waiting for transfers between devices: 104 us -> 80.2 us
  between operations: 14.3 us -> 0.75 us
  local copies, waits for them, and re-layouts: 21.2 us -> 14.5 us
  Pallas kernels: 46.9 us -> 53.5 us
  starting transfers between devices: 15.7 us -> 22 us
  other arithmetic: 10.8 us -> 5.43 us
    all_to_all x1, waiting for transfers between devices: 85.2 us -> 0.01 us  [body(): lax.all_to_all(tiles_b, 'src', split_axis=0, concat_axis=0, tiled=True)]
    ppermute x6 -> x10, waiting for transfers between devices: 3.18 us -> 80.2 us  [exchange(): return lax.ppermute(x, axis, [(a, a ^ flip) for a in range(size)])]
    reduce_scatter x1 -> x0, waiting for transfers between devices: 15.1 us -> none  [body(): projected = lax.psum_scatter(summed, 'src', scatter_dimension=1, tiled=True)]
    unnamed x12 -> x0, other arithmetic: 6.94 us -> none
    pallas_call x4 -> x5, Pallas kernels: 46.9 us -> 53.5 us  [the longest x2 30.4 us: left_products(): pl.pallas_call(left_kernel, grid=(nsource,), out_shape=jax.ShapeDtypeStru...]
    ppermute x6 -> x10, starting transfers between devices: 3.85 us -> 10.2 us  [exchange(): return lax.ppermute(x, axis, [(a, a ^ flip) for a in range(size)])]
    unnamed x35 -> x20, local copies, waits for them, and re-layouts: 12.9 us -> 6.61 us
    convert_element_type x0 -> x2, other arithmetic: none -> 2.94 us  [the longest x1 1.73 us: sum_rows(): return result.astype(total.dtype)]
  transfers between devices with their start and end apart: 9 -> 12, of which waited for: 4 -> 5; matrix products, arithmetic and copies ran while one was open for 9% -> 6% of each run, Pallas kernels for 22% -> 30%
where the time goes in v2:
time: 177 us; the launch traced here: 176 us
  waiting for transfers between devices  80.2 us (45%)
  Pallas kernels  53.5 us (30%)
  starting transfers between devices  22 us (12%)
  local copies, waits for them, and re-layouts  14.5 us (8%)
  other arithmetic  5.43 us (3%)
    ppermute x10, waiting for transfers between devices, exchange(): return lax.ppermute(x, axis, [(a, a ^ flip) for a in range(size)])  80.2 us
    pallas_call x2, Pallas kernels, left_products(): pl.pallas_call(left_kernel, grid=(nsource,), out_shape=jax.ShapeDtypeStru...  30.4 us
    pallas_call x2, Pallas kernels, tiles_and_sums(): pl.pallas_call(functools.partial(tile_kernel, nshard, first, has_start),...  19.9 us
    ppermute x10, starting transfers between devices, exchange(): return lax.ppermute(x, axis, [(a, a ^ flip) for a in range(size)])  10.2 us
    unnamed x20, local copies, waits for them, and re-layouts  6.61 us
    all_to_all x1, starting transfers between devices, body(): lax.all_to_all(tiles_b, 'src', split_axis=0, concat_axis=0, tiled=True)  5.97 us
    all_to_all x1, starting transfers between devices, body(): lax.all_to_all(tiles_a, 'src', split_axis=0, concat_axis=0, tiled=True)  5.82 us
  transfers between devices with their start and end apart: 12, of which 5 were waited for; matrix products, arithmetic and copies ran while one was open for 6% of the time, Pallas kernels for 30%

profile of v2, /device:TPU:0, one launch (start us, length us, event | category | flops | bytes accessed | tf_op | source)
XLA Modules:
  0.0 176.4 jit_solution(10185687059092231599)
XLA Ops:
  0.6 1.0 slice.6.refs_0_
  1.7 0.0 copy-start.1
  1.7 3.0 %collective-permute-start = (bf16[2,256,384]{2,1,0:T(8,128)(2,1)S(1)}, bf16[2,256,384]{2,1,0:T(8,128)(2,1)S(1)}, u32[]{:S(2)}, u32[]{:S(2)}) collective-permute-start(bf16[2,256,384]{2,1,0:T(8,128)(2,1)S(1)} %slice.6.refs_0_), channel_id=1, source_target_pairs={{0,16},{8,24},{16,0},{24,8},{1,17},{9,25},{17,1},{25,9},{2,18},{10... | collective-permute-start | bytes 1179656 | tf_op jit(solution)/shard_map/ppermute | solution.py:17
  4.7 0.0 collective-permute-start.1
  4.7 0.8 constant_dynamic-slice_fusion.3
  5.6 1.4 copy.20.test_ref
  7.0 2.6 %copy.21 = bf16[2,1024,384]{1,2,0:T(8,128)(2,1)} copy(bf16[2,1024,384]{2,1,0:T(8,128)(2,1)} %param.8) | data formatting | bytes 3145728 | tf_op args[1]
  9.6 0.7 pad_maximum_fusion.source_ref
  10.3 3.2 %shard_map.86 = (bf16[2,1024,128]{2,1,0:T(8,128)(2,1)}, bf16[8,128,1024]{2,1,0:T(8,128)(2,1)}) custom-call(f32[2,3,1024]{2,1,0:T(4,128)} %copy.20.test_ref, f32[8,3,1024]{2,1,0:T(4,128)} %pad_maximum_fusion.source_ref), custom_call_target="tpu_custom_call" | custom-call | tf_op jit(solution)/shard_map/pallas_call | solution.py:82
  13.5 9.1 %shard_map.87.left_ref = bf16[2,2,384,1024]{3,2,1,0:T(8,128)(2,1)} custom-call(bf16[2,1024,128]{2,1,0:T(8,128)(2,1)} %get-tuple-element.14.test_ref, bf16[8,128,1024]{2,1,0:T(8,128)(2,1)} %get-tuple-element.20.source_ref, bf16[2,384,1024]{2,1,0:T(8,128)(2,1)} %bitcast.24), custom_call_target="tpu_custom_call" | custom-call | flops 3221225472 | bytes 3145728 | tf_op jit(solution)/shard_map/pallas_call | solution.py:121
  22.6 0.0 collective-permute-done.refs_2_
  22.6 0.6 collective-permute-start.2
  23.2 0.1 slice.7.refs_0_
  23.3 0.0 copy-start.4
  23.3 0.1 collective-permute-start.3
  23.5 0.0 collective-permute-start.4
  23.5 0.0 collective-permute-done.1.refs_1_
  23.5 1.0 collective-permute-done.2.refs_3_
  24.5 0.7 copy-done.6
  25.3 6.2 %shard_map.88 = (bf16[8,2,2,48,384]{4,3,2,1,0:T(8,128)(2,1)}, f32[768,512]{1,0:T(8,128)}) custom-call(s32[2]{0:T(128)} %test_counts_ref.3, s32[8]{0:T(128)} %source_counts_ref.3, bf16[2,2,384,1024]{3,2,1,0:T(8,128)(2,1)} %shard_map.87.left_ref, bf16[2,256,384]{2,1,0:T(8,128)(2,1)} %copy-done.1, bf16[2,256,384]{2,1,0:T(8,128)(2,1)} %collective-permute-done.1.refs_1_, ...), custom_call_target="tpu_custom_call" | custom-call | flops 1811939328 | bytes 4325376 | tf_op jit(solution)/shard_map/pallas_call | solution.py:196
  31.5 0.0 copy-done.4
  31.5 5.8 %all-to-all-start = ((bf16[8,2,2,48,384]{4,3,2,1,0:T(8,128)(2,1)}), bf16[8,2,2,48,384]{4,3,2,1,0:T(8,128)(2,1)S(1)}, u32[]{:S(2)}, u32[]{:S(2)}) async-start(bf16[8,2,2,48,384]{4,3,2,1,0:T(8,128)(2,1)} %get-tuple-element.18), calls=%async_computation | async-start | bytes 2359296 | tf_op jit(solution)/shard_map/all_to_all | solution.py:263
  37.3 21.3 %shard_map.89.left_ref = bf16[2,6,384,1024]{3,2,1,0:T(8,128)(2,1)} custom-call(bf16[2,1024,128]{2,1,0:T(8,128)(2,1)} %get-tuple-element.14.test_ref, bf16[8,128,1024]{2,1,0:T(8,128)(2,1)} %get-tuple-element.20.source_ref, bf16[2,384,1024]{2,1,0:T(8,128)(2,1)} %bitcast.25), custom_call_target="tpu_custom_call" | custom-call | flops 9663676416 | bytes 9437184 | tf_op jit(solution)/shard_map/pallas_call | solution.py:121
  58.7 0.0 collective-permute-done.3.refs_2_
  58.7 0.1 collective-permute-start.5
  58.7 0.0 collective-permute-done.4.refs_1_
  58.7 3.1 %collective-permute-done.5.refs_3_ = bf16[6,256,384]{2,1,0:T(8,128)(2,1)} collective-permute-done((bf16[6,256,384]{2,1,0:T(8,128)(2,1)}, bf16[6,256,384]{2,1,0:T(8,128)(2,1)}, u32[]{:S(2)}, u32[]{:S(2)}) %collective-permute-start.5) | collective-permute-done | bytes 1179680 | tf_op jit(solution)/shard_map/ppermute | solution.py:17
  61.9 13.7 %shard_map.90 = (bf16[8,2,6,48,384]{4,3,2,1,0:T(8,128)(2,1)}, bf16[8,2,48,512]{3,2,1,0:T(8,128)(2,1)}) custom-call(s32[2]{0:T(128)} %test_counts_ref.3, s32[8]{0:T(128)} %source_counts_ref.3, bf16[2,6,384,1024]{3,2,1,0:T(8,128)(2,1)} %shard_map.89.left_ref, bf16[6,256,384]{2,1,0:T(8,128)(2,1)} %copy-done.4, ...), custom_call_target="tpu_custom_call" | custom-call | flops 5435817984 | bytes 12976128 | tf_op jit(solution)/shard_map/pallas_call | solution.py:196
  75.5 0.0 all-to-all-done
  75.5 0.0 copy-start
  75.6 1.0 copy-done
  76.6 6.0 %all-to-all-start.1 = ((bf16[8,2,6,48,384]{4,3,2,1,0:T(8,128)(2,1)}), bf16[8,2,6,48,384]{4,3,2,1,0:T(8,128)(2,1)S(1)}, u32[]{:S(2)}, u32[]{:S(2)}) async-start(bf16[8,2,6,48,384]{4,3,2,1,0:T(8,128)(2,1)} %get-tuple-element.24), calls=%async_computation.1 | async-start | bytes 7077888 | tf_op jit(solution)/shard_map/all_to_all | solution.py:273
  82.6 1.8 %dynamic-slice_bitcast_fusion = bf16[4,2,48,512]{3,2,1,0:T(8,128)(2,1)} fusion(bf16[4,2,2,48,512]{4,3,2,1,0:T(8,128)(2,1)} %bitcast.26, s32[]{:T(128)S(6)} %select_n.50), kind=kLoop, calls=%fused_computation.4 | loop fusion | bytes 786436 | tf_op jit(solution)/shard_map/jit(dynamic_index_in_dim)/squeeze | solution.py:35
  84.4 2.0 %collective-permute-start.6 = (bf16[4,2,48,512]{3,2,1,0:T(8,128)(2,1)}, bf16[4,2,48,512]{3,2,1,0:T(8,128)(2,1)}, u32[]{:S(2)}, u32[]{:S(2)}) collective-permute-start(bf16[4,2,48,512]{3,2,1,0:T(8,128)(2,1)} %dynamic-slice_bitcast_fusion), channel_id=1, source_target_pairs={{0,1},{1,0},{2,3},{3,2},{4,5},{5,4},{6,7},{7,6},{8,9},{9,8},{10,11... | collective-permute-start | bytes 1179656 | tf_op jit(solution)/shard_map/ppermute | solution.py:17
  86.4 34.7 %collective-permute-done.6 = bf16[4,2,48,512]{3,2,1,0:T(8,128)(2,1)} collective-permute-done((bf16[4,2,48,512]{3,2,1,0:T(8,128)(2,1)}, bf16[4,2,48,512]{3,2,1,0:T(8,128)(2,1)}, u32[]{:S(2)}, u32[]{:S(2)}) %collective-permute-start.6) | collective-permute-done | bytes 393248 | tf_op jit(solution)/shard_map/ppermute | solution.py:17
  121.0 1.2 fusion
  122.3 0.7 copy-done.3
  123.0 0.7 dynamic-slice_bitcast_fusion.3
  123.7 0.7 collective-permute-start.7
  124.4 2.1 %collective-permute-start.8 = (bf16[2,48,512]{2,1,0:T(8,128)(2,1)}, bf16[2,48,512]{2,1,0:T(8,128)(2,1)}, u32[]{:S(2)}, u32[]{:S(2)}) collective-permute-start(bf16[2,48,512]{2,1,0:T(8,128)(2,1)} %get-tuple-element.28), channel_id=1, source_target_pairs={{0,4},{1,5},{2,6},{3,7},{4,0},{5,1},{6,2},{7,3},{8,12},{9,13},{10,... | collective-permute-start | bytes 294920 | tf_op jit(solution)/shard_map/ppermute | solution.py:17
  126.5 1.6 collective-permute-start.9
  128.1 16.1 %collective-permute-done.7 = bf16[2,48,512]{2,1,0:T(8,128)(2,1)} collective-permute-done((bf16[2,48,512]{2,1,0:T(8,128)(2,1)}, bf16[2,48,512]{2,1,0:T(8,128)(2,1)}, u32[]{:S(2)}, u32[]{:S(2)}) %collective-permute-start.7) | collective-permute-done | bytes 98336 | tf_op jit(solution)/shard_map/ppermute | solution.py:17
  144.2 25.3 %collective-permute-done.8 = bf16[2,48,512]{2,1,0:T(8,128)(2,1)} collective-permute-done((bf16[2,48,512]{2,1,0:T(8,128)(2,1)}, bf16[2,48,512]{2,1,0:T(8,128)(2,1)}, u32[]{:S(2)}, u32[]{:S(2)}) %collective-permute-start.8) | collective-permute-done | bytes 98336 | tf_op jit(solution)/shard_map/ppermute | solution.py:17
  169.4 0.0 collective-permute-done.9
  169.5 1.7 fusion.3
  171.2 0.0 all-to-all-done.1
  171.2 1.8 %maximum_bitcast_fusion = bf16[2,48,8,8,384]{4,1,3,0,2:T(8,128)(2,1)S(1)} fusion(bf16[8,2,6,48,384]{4,3,2,1,0:T(8,128)(2,1)S(1)} %all-to-all-done.1, bf16[8,2,2,48,384]{4,3,2,1,0:T(8,128)(2,1)} %copy-done), kind=kLoop, calls=%fused_computation | loop fusion | flops 2359296 | bytes 9437184 | tf_op jit(solution)/shard_map/transpose | solution.py:275
  173.0 3.4 %copy.30 = bf16[2,48,8,8,384]{4,3,2,1,0:T(8,128)(2,1)} copy(bf16[2,48,8,8,384]{4,1,3,0,2:T(8,128)(2,1)S(1)} %maximum_bitcast_fusion) | data formatting | bytes 9437184 | tf_op jit(solution)/shard_map/transpose | solution.py:275
  (11 shorter events, 0.1 us)
Async XLA Ops:
  1.7 20.9 %copy-start.1 = (bf16[2,256,384]{2,1,0:T(8,128)(2,1)}, bf16[2,256,384]{2,1,0:T(8,128)(2,1)S(1)}, u32[]{:S(2)}) copy-start(bf16[2,256,384]{2,1,0:T(8,128)(2,1)S(1)} %slice.6.refs_0_) | copy-start | bytes 1179652
  1.7 20.9 %collective-permute-start = (bf16[2,256,384]{2,1,0:T(8,128)(2,1)S(1)}, bf16[2,256,384]{2,1,0:T(8,128)(2,1)S(1)}, u32[]{:S(2)}, u32[]{:S(2)}) collective-permute-start(bf16[2,256,384]{2,1,0:T(8,128)(2,1)S(1)} %slice.6.refs_0_), channel_id=1, source_target_pairs={{0,16},{8,24},{16,0},{24,8},{1,17},{9,25},{17,1},{25,9},{2,18},{10... | collective-permute-start | bytes 1179656 | tf_op jit(solution)/shard_map/ppermute | solution.py:17
  4.7 18.8 %collective-permute-start.1 = (bf16[2,256,384]{2,1,0:T(8,128)(2,1)S(1)}, bf16[2,256,384]{2,1,0:T(8,128)(2,1)}, u32[]{:S(2)}, u32[]{:S(2)}) collective-permute-start(bf16[2,256,384]{2,1,0:T(8,128)(2,1)S(1)} %slice.6.refs_0_), channel_id=1, source_target_pairs={{0,8},{8,0},{16,24},{24,16},{1,9},{9,1},{17,25},{25,17},{2,10},{10... | collective-permute-start | bytes 1179656 | tf_op jit(solution)/shard_map/ppermute | solution.py:17
  13.5 9.7 %copy-start.2 = (bf16[8,256,384]{2,1,0:T(8,128)(2,1)S(1)}, bf16[8,256,384]{2,1,0:T(8,128)(2,1)}, u32[]{:S(2)}) copy-start(bf16[8,256,384]{2,1,0:T(8,128)(2,1)} %param.11) | copy-start | bytes 4718596
  22.6 1.9 %copy-start.5 = (bf16[2,256,384]{2,1,0:T(8,128)(2,1)}, bf16[2,256,384]{2,1,0:T(8,128)(2,1)S(1)}, u32[]{:S(2)}) copy-start(bf16[2,256,384]{2,1,0:T(8,128)(2,1)S(1)} %collective-permute-done.refs_2_) | copy-start | bytes 1179652
  22.6 1.9 %collective-permute-start.2 = (bf16[2,256,384]{2,1,0:T(8,128)(2,1)S(1)}, bf16[2,256,384]{2,1,0:T(8,128)(2,1)S(1)}, u32[]{:S(2)}, u32[]{:S(2)}) collective-permute-start(bf16[2,256,384]{2,1,0:T(8,128)(2,1)S(1)} %collective-permute-done.refs_2_), channel_id=1, source_target_pairs={{0,8},{8,0},{16,24},{24,16},{1,9},{9,1},{17,25},{25,17},{2,10},{10... | collective-permute-start | bytes 1179656 | tf_op jit(solution)/shard_map/ppermute | solution.py:17
  23.3 8.2 %copy-start.4 = (bf16[6,256,384]{2,1,0:T(8,128)(2,1)}, bf16[6,256,384]{2,1,0:T(8,128)(2,1)S(1)}, u32[]{:S(2)}) copy-start(bf16[6,256,384]{2,1,0:T(8,128)(2,1)S(1)} %slice.7.refs_0_) | copy-start | bytes 3538948
  23.3 35.4 %collective-permute-start.3 = (bf16[6,256,384]{2,1,0:T(8,128)(2,1)S(1)}, bf16[6,256,384]{2,1,0:T(8,128)(2,1)}, u32[]{:S(2)}, u32[]{:S(2)}) collective-permute-start(bf16[6,256,384]{2,1,0:T(8,128)(2,1)S(1)} %slice.7.refs_0_), channel_id=1, source_target_pairs={{0,16},{8,24},{16,0},{24,8},{1,17},{9,25},{17,1},{25,9},{2,18},{10... | collective-permute-start | bytes 3538952 | tf_op jit(solution)/shard_map/ppermute | solution.py:17
  23.5 35.3 %collective-permute-start.4 = (bf16[6,256,384]{2,1,0:T(8,128)(2,1)S(1)}, bf16[6,256,384]{2,1,0:T(8,128)(2,1)}, u32[]{:S(2)}, u32[]{:S(2)}) collective-permute-start(bf16[6,256,384]{2,1,0:T(8,128)(2,1)S(1)} %slice.7.refs_0_), channel_id=1, source_target_pairs={{0,8},{8,0},{16,24},{24,16},{1,9},{9,1},{17,25},{25,17},{2,10},{10... | collective-permute-start | bytes 3538952 | tf_op jit(solution)/shard_map/ppermute | solution.py:17
  24.5 0.7 copy-start.6
  31.5 44.0 %all-to-all-start = ((bf16[8,2,2,48,384]{4,3,2,1,0:T(8,128)(2,1)}), bf16[8,2,2,48,384]{4,3,2,1,0:T(8,128)(2,1)S(1)}, u32[]{:S(2)}, u32[]{:S(2)}) async-start(bf16[8,2,2,48,384]{4,3,2,1,0:T(8,128)(2,1)} %get-tuple-element.18), calls=%async_computation | async-start | bytes 2359296 | tf_op jit(solution)/shard_map/all_to_all | solution.py:263
  58.7 3.2 %collective-permute-start.5 = (bf16[6,256,384]{2,1,0:T(8,128)(2,1)}, bf16[6,256,384]{2,1,0:T(8,128)(2,1)}, u32[]{:S(2)}, u32[]{:S(2)}) collective-permute-start(bf16[6,256,384]{2,1,0:T(8,128)(2,1)} %collective-permute-done.3.refs_2_), channel_id=1, source_target_pairs={{0,8},{8,0},{16,24},{24,16},{1,9},{9,1},{17,25},{25,17},{2,10},{10... | collective-permute-start | bytes 3538952 | tf_op jit(solution)/shard_map/ppermute | solution.py:17
  75.5 1.0 copy-start
  76.6 94.6 %all-to-all-start.1 = ((bf16[8,2,6,48,384]{4,3,2,1,0:T(8,128)(2,1)}), bf16[8,2,6,48,384]{4,3,2,1,0:T(8,128)(2,1)S(1)}, u32[]{:S(2)}, u32[]{:S(2)}) async-start(bf16[8,2,6,48,384]{4,3,2,1,0:T(8,128)(2,1)} %get-tuple-element.24), calls=%async_computation.1 | async-start | bytes 7077888 | tf_op jit(solution)/shard_map/all_to_all | solution.py:273
  84.4 36.7 %collective-permute-start.6 = (bf16[4,2,48,512]{3,2,1,0:T(8,128)(2,1)}, bf16[4,2,48,512]{3,2,1,0:T(8,128)(2,1)}, u32[]{:S(2)}, u32[]{:S(2)}) collective-permute-start(bf16[4,2,48,512]{3,2,1,0:T(8,128)(2,1)} %dynamic-slice_bitcast_fusion), channel_id=1, source_target_pairs={{0,1},{1,0},{2,3},{3,2},{4,5},{5,4},{6,7},{7,6},{8,9},{9,8},{10,11... | collective-permute-start | bytes 1179656 | tf_op jit(solution)/shard_map/ppermute | solution.py:17
  122.3 0.7 copy-start.3
  123.7 20.5 %collective-permute-start.7 = (bf16[2,48,512]{2,1,0:T(8,128)(2,1)}, bf16[2,48,512]{2,1,0:T(8,128)(2,1)}, u32[]{:S(2)}, u32[]{:S(2)}) collective-permute-start(bf16[2,48,512]{2,1,0:T(8,128)(2,1)} %get-tuple-element.26), channel_id=1, source_target_pairs={{0,2},{1,3},{2,0},{3,1},{4,6},{5,7},{6,4},{7,5},{8,10},{9,11},{10,... | collective-permute-start | bytes 294920 | tf_op jit(solution)/shard_map/ppermute | solution.py:17
  124.4 45.1 %collective-permute-start.8 = (bf16[2,48,512]{2,1,0:T(8,128)(2,1)}, bf16[2,48,512]{2,1,0:T(8,128)(2,1)}, u32[]{:S(2)}, u32[]{:S(2)}) collective-permute-start(bf16[2,48,512]{2,1,0:T(8,128)(2,1)} %get-tuple-element.28), channel_id=1, source_target_pairs={{0,4},{1,5},{2,6},{3,7},{4,0},{5,1},{6,2},{7,3},{8,12},{9,13},{10,... | collective-permute-start | bytes 294920 | tf_op jit(solution)/shard_map/ppermute | solution.py:17
  126.5 43.0 %collective-permute-start.9 = (bf16[2,48,512]{2,1,0:T(8,128)(2,1)}, bf16[2,48,512]{2,1,0:T(8,128)(2,1)}, u32[]{:S(2)}, u32[]{:S(2)}) collective-permute-start(bf16[2,48,512]{2,1,0:T(8,128)(2,1)} %get-tuple-element.27), channel_id=1, source_target_pairs={{0,6},{1,7},{2,4},{3,5},{4,2},{5,3},{6,0},{7,1},{8,14},{9,15},{10,... | collective-permute-start | bytes 294920 | tf_op jit(solution)/shard_map/ppermute | solution.py:17
